TPU v7x, 32 devices: a whole 2x2x4 slice. The times are simulated.
32 devices in a mesh: dp: 8 (over z, x), seq: 4 (over y, core).
Axes of the slice: x: 2, y: 2, z: 4, core: 2. Of those that a mesh axis runs over, the one named last changes fastest.
Arguments:
- hidden_in: bfloat16 [8, 1024, 768], P('dp', 'seq'), may hold values from -6 to 6
- condition: bfloat16 [8, 256], P('dp'), may hold values from -6 to 6
- qkv_weight: bfloat16 [768, 2304], P('dp'), may hold values from -0.21875 to 0.21875
- out_weight: bfloat16 [768, 768], P('dp'), may hold values from -3.5 to 3.5
- gate_up_weight: bfloat16 [768, 6144], P('dp'), may hold values from -0.21875 to 0.21875
- down_weight: bfloat16 [3072, 768], P('dp'), may hold values from -0.109375 to 0.109375
- ada_weight: bfloat16 [256, 4608], P('dp'), may hold values from -0.375 to 0.375
- pair_embed: bfloat16 [66, 256], replicated, may hold values from -6 to 6
- pair_gain: bfloat16 [256], replicated, may hold values from 0.099609375 to 1.8984375
- pair_weight: bfloat16 [256, 12], replicated, may hold values from -0.375 to 0.375
- valid_len: int32 [8], P('dp'), may hold values from 512 to 1024, as said below
- chain_break: int32 [8], P('dp'), may hold values from 256 to 1535
- out_grad: bfloat16 [8, 1024, 768], P('dp', 'seq'), may hold values from -6 to 6
Outputs:
- result: bfloat16 [8, 1024, 768], P('dp', 'seq')
- input_grad: bfloat16 [8, 1024, 768], P('dp', 'seq')
- grad_qkv: float32 [768, 2304], P('dp')
- grad_out: float32 [768, 768], P('dp')
- grad_gate_up: float32 [768, 6144], P('dp')
- grad_down: float32 [3072, 768], P('dp')
- grad_ada: float32 [256, 4608], P('dp')
- grad_embed: float32 [66, 256], replicated
- grad_gain: float32 [256], replicated
- grad_pair: float32 [256, 12], replicated
Inputs may be any that keep to these rules, and one draw needn't show every extreme that they name: Positions from valid_len on are padding keys; in each aligned group of 1 items one item has live residues in the last residue block of the seq axis; the first item has all 1024 residues. Positions from chain_break on form a second chain; a value of 1024 or more means one chain.
All inputs are finite; a program needn't handle non-finite values.
Results may differ from a plain program's by a relative error of at most 0.023.
Values may be sent and summed in bfloat16 or wider, within the bound.
A program may use at most 192 MiB of HBM per device.

v0:
```python
import functools
import types

import jax
import jax.numpy as jnp
from jax import lax
from jax.experimental import pallas as pl
from jax.experimental.pallas import tpu as pltpu
from jax.sharding import PartitionSpec as P

H = 12
DH = 64
RR = 32
CLASSES = 66

HIGHEST = lax.Precision.HIGHEST
F32 = jnp.float32
BF16 = jnp.bfloat16


VMEM_LIMIT = 65400 * 2**10


def layer_norm(values, epsilon=1e-06):
    average = jnp.mean(values, axis=-1, keepdims=True)
    centered = values - average
    inv_std = lax.rsqrt(jnp.mean(centered * centered, axis=-1, keepdims=True) + epsilon)
    return (centered * inv_std, inv_std)


def norm_back(upstream, normal, inv_std):
    return inv_std * (
        upstream
        - jnp.mean(upstream, axis=-1, keepdims=True)
        - normal * jnp.mean(upstream * normal, axis=-1, keepdims=True)
    )


def pair_table(pair_embed, pair_gain, pair_weight):
    average = jnp.mean(pair_embed, axis=-1, keepdims=True)
    centered = pair_embed - average
    normal = centered * lax.rsqrt(jnp.mean(centered * centered, axis=-1, keepdims=True) + 1e-05)
    return jnp.dot(normal * pair_gain, pair_weight, precision=HIGHEST)


def mm(spec, a, b):
    return jnp.einsum(spec, a, b, preferred_element_type=F32)


def plain_body(
    hidden_in,
    condition,
    qkv_weight,
    out_weight,
    gate_up_weight,
    down_weight,
    ada_weight,
    pair_embed,
    pair_gain,
    pair_weight,
    valid_len,
    chain_break,
    out_grad,
):
    items, rows, width = hidden_in.shape
    seq = lax.axis_size("seq")
    dp = lax.axis_size("dp")
    me = lax.axis_index("seq")
    at = lax.axis_index("dp")
    length = rows * seq
    heads = H // seq
    part = heads * DH
    shard = qkv_weight.shape[0]
    strip = down_weight.shape[0] // seq
    hidden_units = dp * strip

    def pick(array, axis):
        return lax.dynamic_index_in_dim(array, me, axis, keepdims=False)

    def gather(array, name, axis):
        return lax.all_gather(array, name, axis=axis, tiled=True)

    def scatter(array, name, axis):
        return lax.psum_scatter(array, name, scatter_dimension=axis, tiled=True)

    conditions = gather(condition, "dp", 0)
    squashed = jax.nn.silu(conditions.astype(F32)).astype(BF16)
    ada_rows = ada_weight.shape[0]
    squashed_part = lax.dynamic_slice_in_dim(squashed, at * ada_rows, ada_rows, 1)
    modulation = scatter(mm("ic,ce->ie", squashed_part, ada_weight), "dp", 0)
    shift_one, scale_one, gate_one, shift_two, scale_two, gate_two = jnp.split(
        modulation[:, None, :], 6, axis=-1
    )
    qkv_w = gather(pick(qkv_weight.reshape(shard, 3, seq, part), 2).reshape(shard, 3 * part), "dp", 0)
    gate_up_w = gather(
        pick(gate_up_weight.reshape(shard, 2, dp, seq, strip), 3).reshape(shard, 2 * hidden_units), "dp", 0
    )
    down_w = gather(pick(down_weight.reshape(seq, strip, width), 0), "dp", 0)
    out_w = gather(gather(pick(out_weight.reshape(shard, seq, width // seq), 1), "dp", 0), "seq", 1)

    table, pair_pull = jax.vjp(
        pair_table, pair_embed.astype(F32), pair_gain.astype(F32), pair_weight.astype(F32)
    )
    my_table = lax.dynamic_slice_in_dim(table, me * heads, heads, 1)
    spread = jnp.arange(2 * length)
    distance = jnp.where(spread < length, -spread, 2 * length - spread)
    line = jnp.take(my_table, jnp.clip(distance, -RR, RR) + RR, axis=0).T
    toeplitz = jnp.tile(line, (1, length))[:, : length * (2 * length - 1)]
    toeplitz = toeplitz.reshape(heads, length, 2 * length - 1)[:, :, :length]
    positions = jnp.arange(length, dtype=jnp.int32)
    side = positions[None] >= chain_break[:, None]
    same = side[:, :, None] == side[:, None, :]
    alive = (positions[None] < valid_len[:, None])[:, None, None, :]

    hidden = gather(hidden_in, "seq", 1).astype(F32)
    upstream = out_grad.astype(F32)
    first_norm, first_inv = layer_norm(hidden)
    first = (first_norm * (1.0 + scale_one) + shift_one).astype(BF16)
    merged = mm("ird,de->ire", first, qkv_w).astype(BF16)
    queries, keys, values = (
        part_of.reshape(items, length, heads, DH) for part_of in jnp.split(merged, 3, axis=-1)
    )
    logits = mm("iqhd,ikhd->ihqk", queries, keys) * 0.125
    logits = logits + jnp.where(same[:, None], toeplitz[None], my_table[CLASSES - 1][None, :, None, None])
    logits = jnp.where(alive, logits, -1e30)
    powers = jnp.exp(logits - jnp.max(logits, axis=-1, keepdims=True))
    probs = powers / jnp.sum(powers, axis=-1, keepdims=True)
    probs_low = probs.astype(BF16)
    mixed_heads = mm("ihqk,ikhd->iqhd", probs_low, values)
    mixed_part = mixed_heads.reshape(items, length, part).astype(BF16)
    mixed_all = gather(mixed_part, "seq", 2)

    def mine(array):
        return lax.dynamic_slice_in_dim(array, me * rows, rows, 1)

    branch = mm("ire,ed->ird", mine(mixed_all), out_w)
    middle = hidden_in.astype(F32) + gate_one * branch
    second_norm, second_inv = layer_norm(middle)
    second = gather((second_norm * (1.0 + scale_two) + shift_two).astype(BF16), "seq", 1)
    gate_up = mm("ird,de->ire", second, gate_up_w)
    gate_part, up_part = jnp.split(gate_up, 2, axis=-1)
    sigmoid_gate = jax.nn.sigmoid(gate_part)
    inner = (gate_part * sigmoid_gate * up_part).astype(BF16)
    feed = scatter(mm("irf,fd->ird", inner, down_w).astype(BF16), "seq", 1).astype(F32)
    result = (middle + gate_two * feed).astype(BF16)

    feed_grad = (gate_two * gather(out_grad, "seq", 1).astype(F32)).astype(BF16)
    d_gate_two = jnp.sum(upstream * feed, axis=1)
    grad_down = mm("irf,ird->fd", inner, feed_grad)
    inner_grad = mm("ird,fd->irf", feed_grad, down_w)
    gate_grad = inner_grad * up_part * sigmoid_gate * (1.0 + gate_part * (1.0 - sigmoid_gate))
    up_grad = inner_grad * gate_part * sigmoid_gate
    gate_up_grad = jnp.concatenate([gate_grad, up_grad], axis=-1).astype(BF16)
    grad_gate_up = mm("ird,ire->de", second, gate_up_grad)
    second_grad = scatter(mm("ire,de->ird", gate_up_grad, gate_up_w).astype(BF16), "seq", 1).astype(F32)
    d_shift_two = jnp.sum(second_grad, axis=1)
    d_scale_two = jnp.sum(second_grad * second_norm, axis=1)
    middle_grad = upstream + norm_back(second_grad * (1.0 + scale_two), second_norm, second_inv)
    branch_grad = (gate_one * middle_grad).astype(BF16)
    d_gate_one = jnp.sum(middle_grad * branch, axis=1)
    branch_grad_all = gather(branch_grad, "seq", 1)
    my_columns = lax.dynamic_slice_in_dim(branch_grad_all, me * part, part, 2)
    grad_out = mm("ire,ird->ed", mixed_all, my_columns)
    out_w_rows = lax.dynamic_slice_in_dim(out_w, me * part, part, 0)
    mixed_grad = mm("ird,ed->ire", branch_grad_all, out_w_rows).astype(BF16).reshape(items, length, heads, DH)

    prob_grad = mm("iqhd,ikhd->ihqk", mixed_grad, values)
    delta = jnp.sum(probs * prob_grad, axis=-1, keepdims=True)
    score_grad = (probs * (prob_grad - delta)).astype(BF16)
    query_grad = mm("ihqk,ikhd->iqhd", score_grad, keys) * 0.125
    key_grad = mm("ihqk,iqhd->ikhd", score_grad, queries) * 0.125
    value_grad = mm("ihqk,iqhd->ikhd", probs_low, mixed_grad)
    merged_grad = jnp.concatenate(
        [term.reshape(items, length, part) for term in (query_grad, key_grad, value_grad)], axis=-1
    ).astype(BF16)
    wide = score_grad.astype(F32)
    kept = jnp.sum(jnp.where(same[:, None], wide, 0.0), axis=0)
    crossed = jnp.sum(jnp.where(same[:, None], 0.0, wide), axis=(0, 2, 3))
    skewed = jnp.pad(kept[:, :, ::-1], ((0, 0), (0, 0), (0, length))).reshape(heads, -1)
    skewed = skewed[:, : length * (2 * length - 1)].reshape(heads, length, 2 * length - 1)
    lines = jnp.sum(skewed, axis=1)
    middle_line = length - 1
    low_end = jnp.sum(lines[:, : middle_line - RR + 1], axis=1)
    high_end = jnp.sum(lines[:, middle_line + RR :], axis=1)
    near = lines[:, middle_line - RR + 1 : middle_line + RR]
    my_table_grad = jnp.concatenate([low_end[:, None], near, high_end[:, None], crossed[:, None]], axis=1).T
    table_grad = lax.psum(
        lax.dynamic_update_slice_in_dim(jnp.zeros((CLASSES, H), F32), my_table_grad, me * heads, 1), ("dp", "seq")
    )
    grad_embed, grad_gain, grad_pair = pair_pull(table_grad)

    grad_qkv = mm("ird,ire->de", first, merged_grad)
    first_grad = scatter(mm("ire,de->ird", merged_grad, qkv_w).astype(BF16), "seq", 1).astype(F32)
    my_norm, my_inv = mine(first_norm), mine(first_inv)
    d_shift_one = jnp.sum(first_grad, axis=1)
    d_scale_one = jnp.sum(first_grad * my_norm, axis=1)
    input_grad = middle_grad + norm_back(first_grad * (1.0 + scale_one), my_norm, my_inv)
    modulation_grad = jnp.concatenate(
        [d_shift_one, d_scale_one, d_gate_one, d_shift_two, d_scale_two, d_gate_two], axis=-1
    )
    modulation_grads = gather(lax.psum(modulation_grad, "seq"), "dp", 0)
    grad_ada = jnp.einsum("ic,ie->ce", squashed_part.astype(F32), modulation_grads, precision=HIGHEST)

    def owned(grad):
        return scatter(grad.astype(BF16), "dp", 0)

    def everyone(grad):
        return lax.all_gather(grad, "seq", axis=0)

    shares_qkv = everyone(owned(grad_qkv)).reshape(seq, shard, 3, part)
    shares_out = everyone(owned(grad_out))
    shares_gate_up = everyone(owned(grad_gate_up)).reshape(seq, shard, 2, dp, strip)
    shares_down = everyone(owned(grad_down))
    return (
        result,
        input_grad.astype(BF16),
        jnp.transpose(shares_qkv, (1, 2, 0, 3)).reshape(shard, -1).astype(F32),
        jnp.transpose(shares_out, (1, 0, 2)).reshape(shard, -1).astype(F32),
        jnp.transpose(shares_gate_up, (1, 2, 3, 0, 4)).reshape(shard, -1).astype(F32),
        shares_down.reshape(seq * strip, width).astype(F32),
        grad_ada,
        grad_embed,
        grad_gain,
        grad_pair,
    )


MESH = pl.DeviceIdType.MESH
LANES = 128


def nn(a, b):
    return jnp.dot(a, b, preferred_element_type=F32)


def nt(a, b):
    return lax.dot_general(a, b, (((1,), (1,)), ((), ())), preferred_element_type=F32)


def tn(a, b):
    return lax.dot_general(a, b, (((0,), (0,)), ((), ())), preferred_element_type=F32)


def skew(tile, back):
    row = lax.broadcasted_iota(jnp.int32, tile.shape, 0)
    for bit in range(7):
        turn = LANES - (1 << bit) if back else 1 << bit
        tile = jnp.where(((row >> bit) & 1) == 1, pltpu.roll(tile, turn, 1), tile)
    return tile


class Sizes:
    def __init__(self, rows, width, seq, dp, shard, down_shard, ada_rows, conditioning):
        self.rows, self.width, self.seq, self.dp = rows, width, seq, dp
        self.shard, self.ada_rows, self.conditioning = shard, ada_rows, conditioning
        self.strip = down_shard // seq
        self.length = rows * seq
        self.heads = H // seq
        self.part = self.heads * DH
        self.hidden = self.strip * dp
        self.far = dp // 2
        self.half = shard // 2
        self.blocks = self.length // LANES


def under(where, work):
    if where is None:
        work()
    else:
        pl.when(where)(work)


class Wires:
    def __init__(self, send, recv):
        self.send, self.recv, self.count, self.started = send, recv, 0, []

    def reserve(self, count=1):
        first = self.count
        self.count += count
        return first

    def make(self, number, source, target, device):
        return pltpu.make_async_remote_copy(
            src_ref=source,
            dst_ref=target,
            send_sem=self.send.at[number],
            recv_sem=self.recv.at[number],
            device_id=device,
            device_id_type=MESH,
        )

    def go(self, number, source, target, device, where=None):
        copy = self.make(number, source, target, device)
        under(where, copy.start)
        self.started.append((copy, where))
        return copy

    def settle(self, copy):
        copy.wait_send()
        self.started = [other for other in self.started if other[0] is not copy]

    def finish(self):
        for copy, where in self.started:
            under(where, copy.wait_send)
        self.started = []


def layer_kernel(sizes, names, *refs):
    r = types.SimpleNamespace(**dict(zip(names, refs, strict=True)))
    n = sizes
    rows, width, part, heads, length, hid = n.rows, n.width, n.part, n.heads, n.length, n.hidden
    half_rows = rows // 2
    d, s = lax.axis_index("dp"), lax.axis_index("seq")
    z, x = d // 2, lax.rem(d, 2)
    y, c = s // 2, lax.rem(s, 2)
    ox, oy, oc = 1 - x, 1 - y, 1 - c
    at_x = (z * 2 + ox, s)
    at_y = (d, oy * 2 + c)
    at_c = (d, y * 2 + oc)

    def z_plus(k):
        return lax.rem(z + k, n.far)

    def at_z(k):
        return (z_plus(k) * 2 + x, s)

    wires = Wires(r.send_sem, r.recv_sem)
    dp_peers = [(k, e) for k in range(n.far) for e in range(2) if k or e]
    seq_peers = [(1, 0), (0, 1), (1, 1)]

    def dp_peer(k, e):
        xx = lax.rem(x + e, 2)
        return z_plus(k) * 2 + xx, lax.rem(z + n.far - k, n.far) * 2 + xx

    def seq_peer(a, b):
        return lax.rem(y + a, 2) * 2 + lax.rem(c + b, 2)

    local_count = [0]

    def local(source, target):
        copy = pltpu.make_async_copy(source, target, r.local_sem.at[local_count[0]])
        local_count[0] += 1
        copy.start()
        return copy

    qkv_stage, gate_up_stage = r.second_t, r.gate_up_grads
    staged = [
        local(r.qkv.at[:, q * width : (q + 1) * width], qkv_stage.at[q * n.shard : (q + 1) * n.shard, 0:width])
        for q in range(3)
    ]
    staged_gate_up = [
        local(r.gate_up.at[:, q * 2 * hid : (q + 1) * 2 * hid], gate_up_stage.at[q * n.shard : (q + 1) * n.shard])
        for q in range(n.seq)
    ]
    own_shard = pl.ds(pl.multiple_of(d * n.shard, n.shard), n.shard)
    r.cond_all[d] = jnp.broadcast_to(r.condition[...].astype(F32), (8, n.conditioning))
    barrier = pltpu.get_barrier_semaphore()
    for k, e in dp_peers:
        pl.semaphore_signal(barrier, inc=1, device_id=(dp_peer(k, e)[0], s), device_id_type=MESH)
    for a, b in seq_peers:
        pl.semaphore_signal(barrier, inc=1, device_id=(d, seq_peer(a, b)), device_id_type=MESH)
    for copy in staged:
        copy.wait()
    for side in range(n.seq):

        @pl.when(s == side)
        def _():
            r.w_qkv[own_shard, :] = jnp.concatenate(
                [
                    qkv_stage[q * n.shard : (q + 1) * n.shard, side * part + h * DH : side * part + (h + 1) * DH]
                    for h in range(heads)
                    for q in range(3)
                ],
                axis=1,
            )

    pl.semaphore_wait(barrier, len(dp_peers) + len(seq_peers))

    class SeqGather:
        def __init__(self, block):
            self.block, self.first = block, wires.reserve(3)
            self.mine, self.from_y, self.from_c, self.from_yc = s, at_y[1], at_c[1], oy * 2 + oc

        def start(self, source=None):
            mine = self.block(self.mine)
            source = mine if source is None else source
            self.sent = [wires.go(self.first, source, mine, at_y), wires.go(self.first + 1, source, mine, at_c)]

        def hand_on(self):
            place = self.block(self.from_y)
            wires.make(self.first, place, place, at_y).wait_recv()
            self.sent.append(wires.go(self.first + 2, place, place, at_c))

        def settle(self):
            for copy in self.sent:
                wires.settle(copy)

        def wait_core(self):
            place = self.block(self.from_c)
            wires.make(self.first + 1, place, place, at_c).wait_recv()

        def wait_last(self):
            place = self.block(self.from_yc)
            wires.make(self.first + 2, place, place, at_c).wait_recv()

        def wait(self):
            self.hand_on()
            self.wait_core()
            self.wait_last()

    last_z = n.far - 1

    class Wave:
        def __init__(self, block, direct=False):
            self.block, self.first, self.direct = block, wires.reserve(4), direct

        def send(self, source=None):
            mine = self.block(z)
            source = mine if source is None else source
            wires.go(self.first + 1, source, mine, at_z(1), None if self.direct else z != last_z)
            wires.go(self.first + 3, source, mine, at_z(3), None if self.direct else z != 0)
            wires.go(self.first + 2, source, mine, at_z(2))

        def relay(self):
            place = self.block(z_plus(2))
            wires.make(self.first + 2, place, place, at_z(2)).wait_recv()
            if not self.direct:
                wires.go(self.first, place, place, at_z(1), z == last_z - 1)
                wires.go(self.first, place, place, at_z(3), z == 1)

        def arrive(self, k):
            place = self.block(z_plus(n.far - k))
            far_end = z == (0 if k == 1 else last_z)
            near = wires.make(self.first + k, place, place, at_z(k))
            if self.direct:
                near.wait_recv()
                return
            far = wires.make(self.first, place, place, at_z(k))
            under(far_end, far.wait_recv)
            under(jnp.logical_not(far_end), near.wait_recv)

    class DpGather:
        def __init__(self, source, place, direct=False):
            self.source, self.place, self.first = source, place, wires.reserve(n.far)
            self.wave = Wave(lambda zz: place(zz * 2 + x), direct)

        def start(self):
            mine = self.place(d)
            self.own = None if self.source is None else local(self.source, mine)
            wires.go(self.first, mine if self.source is None else self.source, mine, at_x)

        def along_z(self):
            self.wave.send(self.source)

        def across(self, k):
            place = self.place(z_plus(n.far - k) * 2 + x)
            wires.go(self.first + k, place, place, at_x)

        def relay(self):
            self.wave.relay()
            self.across(2)

        def hand_on(self):
            for k in (1, 3):
                self.wave.arrive(k)
                self.across(k)

        def wait(self):
            if self.own is not None:
                self.own.wait()
            for k in range(n.far):
                place = self.place(z_plus(n.far - k) * 2 + ox)
                wires.make(self.first + k, place, place, at_x).wait_recv()

    class DpGatherX:
        def __init__(self, source, place):
            self.source, self.place, self.first = source, place, wires.reserve()
            self.waves = Wave(lambda zz: place(zz * 2 + x)), Wave(lambda zz: place(zz * 2 + ox))

        def start(self):
            self.own = local(self.source, self.place(d))
            wires.go(self.first, self.source, self.place(d), at_x)

        def along_z(self):
            self.waves[0].send(self.source)

        def cross(self):
            place = self.place(z * 2 + ox)
            wires.make(self.first, place, place, at_x).wait_recv()
            self.waves[1].send()

        def relay(self, which):
            self.waves[which].relay()

        def wait(self):
            self.own.wait()
            for wave in self.waves:
                wave.arrive(1)
                wave.arrive(3)

    class SeqReduce:
        def __init__(self, sib, got, over, come):
            self.sib, self.got, self.over, self.come = sib, got, over, come
            self.first, self.sent = wires.reserve(3), []

        def put_core(self, index):
            def put(lanes, block):
                self.sib[index, :, lanes] = block.astype(BF16)

            return put

        def to_core(self, index):
            self.sent.append(wires.go(self.first + index, self.sib.at[index], self.got.at[index], at_c))

        def wait_far(self):
            wires.make(self.first + 1, self.sib.at[1], self.got.at[1], at_c).wait_recv()

        def put_y(self):
            def put(lanes, block):
                self.over[:, lanes] = (block + self.got[1, :, lanes].astype(F32)).astype(BF16)

            return put

        def to_y(self):
            self.sent.append(wires.go(self.first + 2, self.over, self.come, at_y))

        def settle(self):
            for copy in self.sent:
                wires.settle(copy)

        def wait(self):
            wires.make(self.first, self.sib.at[0], self.got.at[0], at_c).wait_recv()
            wires.make(self.first + 2, self.over, self.come, at_y).wait_recv()

        def total(self, own, place):
            return own[place, :] + self.got[0, place, :].astype(F32) + self.come[place, :].astype(F32)

    at_end = z * (last_z - z) == 0
    inside = z * (last_z - z) != 0

    def mirror(k):
        return (z, z + 1 - 2 * lax.rem(z, 2), lax.rem(z + 2, n.far), last_z - z)[k]

    def at_mirror(k):
        return (mirror(k) * 2 + x, s)

    def add_up(target, parts):
        def one(q, _):
            place = pl.ds(pl.multiple_of(q * 16, 16), 16)
            total = parts[0][..., place, :].astype(F32)
            for other in parts[1:]:
                total = total + other[..., place, :].astype(F32)
            target[..., place, :] = total.astype(BF16)
            return 0

        lax.fori_loop(0, target.shape[-2] // 16, one, 0)

    class Shares:
        def __init__(self, mine, share):
            self.mine, self.share = mine, share
            self.gather = SeqGather(lambda t: share.at[t])

        def start(self):
            self.own = local(self.mine, self.share.at[s])
            self.gather.start(self.mine)

        def hand_on(self):
            self.gather.hand_on()

        def wait(self):
            self.gather.wait_core()
            self.gather.wait_last()
            self.own.wait()

    class DpReduce:
        def __init__(self, grad, got, come, far, mine, share):
            self.grad, self.got, self.come, self.far, self.mine = grad, got, come, far, mine
            self.first, self.second, self.shares = wires.reserve(n.far), wires.reserve(n.far), Shares(mine, share)

        def start(self):
            for k in (3, 1, 2, 0):
                to = mirror(k)
                wires.go(self.first + k, self.grad.at[ox, to], self.got.at[to], at_x)

        def along_z(self, k):
            to = mirror(k)
            block = self.grad.at[x, to]
            wires.make(self.first + k, self.grad.at[ox, to], self.got.at[to], at_x).wait_recv()
            add_up(block, (block, self.got.at[to]))
            if k == 3:
                wires.go(self.second, block, self.far, at_mirror(1), at_end)
                wires.go(self.second + 3, block, self.come.at[0], at_mirror(3), inside)
            elif k == 1:
                wires.go(self.second + 1, block, self.come.at[2], at_mirror(1))
            elif k == 2:

                @pl.when(inside)
                def _():
                    wires.make(self.second, block, self.far, at_mirror(1)).wait_recv()
                    add_up(block, (block, self.far))

                wires.go(self.second + 2, block, self.come.at[1], at_mirror(2))

        def finish(self):
            for k in (2, 1):
                wires.make(self.second + k, self.mine, self.come.at[3 - k], at_mirror(k)).wait_recv()
            near = self.grad.at[x, z], self.come.at[1], self.come.at[2]

            @pl.when(at_end)
            def _():
                add_up(self.mine, near)

            @pl.when(inside)
            def _():
                wires.make(self.second + 3, self.mine, self.come.at[0], at_mirror(3)).wait_recv()
                add_up(self.mine, (*near, self.come.at[0]))

            self.shares.start()

    class DpReduceZ:
        def __init__(self, grad, come, far, got, mine, share):
            self.grad, self.come, self.far, self.got, self.mine = grad, come, far, got, mine
            self.first, self.cross, self.shares = wires.reserve(4), wires.reserve(), Shares(mine, share)

        def start(self, which):
            ways = (
                (0, self.far, 1, at_end),
                (3, self.come.at[0], 3, inside),
                (1, self.come.at[2], 1, None),
                (2, self.come.at[1], 2, at_end),
            )
            for k, place, to, where in ways[2 * which : 2 * which + 2]:
                block = self.grad.at[:, mirror(k or 3)]
                wires.go(self.first + k, block, place, at_mirror(to), where)

        def merge(self):
            block = self.grad.at[:, mirror(2)]

            @pl.when(inside)
            def _():
                wires.make(self.first, block, self.far, at_mirror(1)).wait_recv()
                add_up(block, (block, self.far))

            wires.go(self.first + 2, block, self.come.at[1], at_mirror(2), inside)

        def across(self):
            block = self.grad.at[:, z]
            for k in (2, 1):
                wires.make(self.first + k, self.far, self.come.at[3 - k], at_mirror(k)).wait_recv()
            near = block, self.come.at[1], self.come.at[2]

            @pl.when(at_end)
            def _():
                add_up(block, near)

            @pl.when(inside)
            def _():
                wires.make(self.first + 3, self.far, self.come.at[0], at_mirror(3)).wait_recv()
                add_up(block, (*near, self.come.at[0]))

            wires.go(self.cross, self.grad.at[ox, z], self.got, at_x)

        def finish(self):
            wires.make(self.cross, self.mine, self.got, at_x).wait_recv()
            add_up(self.mine, (self.grad.at[x, z], self.got))
            self.shares.start()

    step = 64

    def by_rows(count, work, start=0, unroll=2):
        def one(q, carry):
            return work(pl.ds(pl.multiple_of(q * step, step), step), carry)

        return lax.fori_loop(0, count // step, one, start, unroll=unroll)

    wide = 2 * LANES

    def by_lanes(count, work, unroll=True):
        def one(q, _):
            work(pl.ds(pl.multiple_of(q * wide, wide), wide))
            return 0

        lax.fori_loop(0, count // wide, one, 0, unroll=unroll)

    def fold_rows(array):
        return jnp.sum(array.reshape(step // 8, 8, width), axis=0)

    hidden_all, grads_all = r.hidden_all, r.grads_all

    def rows_of(ref):
        return lambda t: ref.at[pl.ds(pl.multiple_of(t * rows, rows), rows)]

    hidden_gather, up_gather = SeqGather(rows_of(hidden_all)), SeqGather(rows_of(grads_all))
    def shard_rows(ref, height, lanes=slice(None)):
        return lambda t: ref.at[pl.ds(pl.multiple_of(t * height, height), height), lanes]

    def lane_half(side):
        return pl.ds(pl.multiple_of(side * (width // 2), width // 2), width // 2)

    lanes_y = lane_half(y)
    qkv_gathers = [
        DpGather(None, shard_rows(r.w_qkv, n.shard, lanes), True)
        for lanes in (slice(0, 2 * LANES), slice(2 * LANES, 3 * part))
    ]
    out_gather = DpGather(
        r.out.at[pl.ds(pl.multiple_of(c * n.half, n.half), n.half), lanes_y],
        lambda t: r.w_out.at[t, c, :, lanes_y],
    )
    half_strip = n.strip // 2

    def down_half(kind, side):
        low = side * half_strip
        return kind(
            r.down.at[pl.ds(pl.multiple_of(s * n.strip + low, half_strip), half_strip)],
            lambda t: r.w_down.at[pl.ds(pl.multiple_of(t * n.strip + low, half_strip), half_strip)],
        )

    down_near, down_gather = down_half(DpGather, 0), down_half(DpGatherX, 1)
    pieces = [
        DpGather(None, shard_rows(r.w_gate_up, n.shard, slice(q * (hid // 2), (q + 1) * (hid // 2))))
        for q in (0, 2, 1, 3)
    ]

    def out_block(t):
        ty, tc = t // 2, lax.rem(t, 2)
        return r.w_out.at[:, tc, :, lane_half(ty)]

    out_share = SeqGather(out_block)

    cond_first, mod_first = wires.reserve(len(dp_peers)), wires.reserve(len(dp_peers))
    cond_all, mod_send, mod_recv = r.cond_all, r.mod_send, r.mod_recv
    for i, (k, e) in enumerate(dp_peers):
        wires.go(cond_first + i, cond_all.at[d], cond_all.at[d], (dp_peer(k, e)[0], s))
    for piece in qkv_gathers:
        piece.along_z()
        piece.start()
    own_hidden = local(r.hidden, hidden_gather.block(s))
    keep_hidden = local(r.hidden, r.hidden_own)
    keep_grads = local(r.out_grad, r.upstream)
    hidden_gather.start(r.hidden)
    own_grads = local(r.out_grad, up_gather.block(s))


    for i, (k, e) in enumerate(dp_peers):
        place = cond_all.at[dp_peer(k, e)[1]]
        wires.make(cond_first + i, place, place, (dp_peer(k, e)[0], s)).wait_recv()
    item_of = lax.broadcasted_iota(jnp.int32, (n.dp, n.conditioning), 0)
    conditions = jnp.where(item_of == 0, cond_all[0], 0.0)
    for i in range(1, n.dp):
        conditions = jnp.where(item_of == i, cond_all[i], conditions)
    squashed = (conditions * (1.0 / (1.0 + jnp.exp(-conditions)))).astype(BF16).astype(F32)
    r.squashed[...] = squashed.T
    squashed_rows = r.squashed[pl.ds(pl.multiple_of(d * n.ada_rows, n.ada_rows), n.ada_rows), :]
    ada_part = tn(squashed_rows.astype(BF16), r.ada[...])
    for i in range(n.dp):
        mod_send[i] = ada_part[i : i + 1]
    mod_recv[d] = mod_send[d]
    for i, (k, e) in enumerate(dp_peers):
        wires.go(mod_first + i, mod_send.at[dp_peer(k, e)[0]], mod_recv.at[d], (dp_peer(k, e)[0], s))
    for copy in staged_gate_up:
        copy.wait()
    group = n.seq * n.strip
    for side in range(n.seq):

        @pl.when(s == side)
        def _():
            strips = []
            for number in range(2 * n.dp):
                block, low = divmod(number * group, 2 * hid)
                low += side * n.strip
                strips.append(gate_up_stage[block * n.shard : (block + 1) * n.shard, low : low + n.strip])
            r.w_gate_up[own_shard, :] = jnp.concatenate(strips, axis=1)

    for piece in (out_gather, *pieces[:2]):
        piece.start()
        piece.along_z()
    down_gather.start()
    down_gather.along_z()
    down_near.start()
    down_near.along_z()
    for piece in pieces[2:]:
        piece.start()
    hidden_gather.hand_on()
    up_gather.start(r.out_grad)
    for piece in qkv_gathers:
        piece.relay()
        piece.hand_on()

    bias, table_t = r.bias, r.table_t
    embed = r.pair_embed[...].astype(F32)
    normal, _ = layer_norm(embed, 1e-05)
    scaled = normal * r.pair_gain[...].astype(F32)
    scaled = jnp.concatenate([scaled, jnp.zeros((LANES - CLASSES, scaled.shape[1]), F32)], axis=0)
    table_t[...] = lax.dot_general(
        r.pair_weight[...].astype(F32),
        scaled,
        (((1,), (1,)), ((), ())),
        precision=HIGHEST,
        preferred_element_type=F32,
    )

    def table_line(h):
        return table_t[pl.ds(s * heads + h, 1), :]

    key_in = lax.broadcasted_iota(jnp.int32, (LANES, LANES), 0)
    query_in = lax.broadcasted_iota(jnp.int32, (LANES, LANES), 1)
    middle_tile = n.blocks - 1

    def build_bias(h, _):
        line = table_line(h)
        near = skew(jnp.broadcast_to(pltpu.roll(line, LANES - RR, 1), (LANES, LANES)), False)
        low_end = jnp.broadcast_to(line[:, 0:1], (LANES, LANES))
        high_end = jnp.broadcast_to(line[:, 2 * RR : 2 * RR + 1], (LANES, LANES))
        for tile in range(2 * n.blocks - 1):
            away = tile - middle_tile
            apart = query_in - key_in - away * LANES
            if away < -1:
                value = high_end
            elif away > 1:
                value = low_end
            else:
                value = jnp.where(apart >= RR, high_end, jnp.where(apart <= -RR, low_end, near))
            bias[h, tile * LANES : (tile + 1) * LANES] = value
        return 0

    lax.fori_loop(0, heads, build_bias, 0)

    own_hidden.wait()
    hidden_gather.wait_core()
    hidden_gather.wait_last()
    for i, (k, e) in enumerate(dp_peers):
        place = mod_recv.at[dp_peer(k, e)[1]]
        wires.make(mod_first + i, mod_send.at[d], place, (dp_peer(k, e)[0], s)).wait_recv()
    modulation = mod_recv[0]
    for i in range(1, n.dp):
        modulation = modulation + mod_recv[i]
    r.modulation[...] = modulation

    def vector(index):
        return r.modulation[:, index * width : (index + 1) * width]

    shift_one, scale_one, gate_one, shift_two, scale_two, gate_two = range(6)
    first = hidden_all
    hidden_gather.settle()

    def make_first(t, _):
        place = pl.ds(pl.multiple_of(t * LANES, LANES), LANES)
        normal, _ = layer_norm(hidden_all[place, :].astype(F32))
        first[place, :] = (normal * (1.0 + vector(scale_one)) + vector(shift_one)).astype(BF16)
        r.norm_t[:, place] = normal.astype(BF16).T
        return 0

    lax.fori_loop(0, n.blocks, make_first, 0)
    few_rows = jnp.concatenate([vector(q) for q in range(6)] + [vector(0)] * 2, axis=0)
    r.mod_t[...] = few_rows.T
    out_gather.relay()
    out_gather.hand_on()
    pieces[0].relay()

    for piece in qkv_gathers:
        piece.wait()
    w_qkv = r.w_qkv
    keys = r.keys
    keys_t, values_t, queries_t = r.keys_t, r.values_t, r.queries_t
    w_qkv_t = r.inner_t

    def turn_weight(q, _):
        place = pl.ds(pl.multiple_of(q * 2 * LANES, 2 * LANES), 2 * LANES)
        w_qkv_t[0 : 3 * part, place] = w_qkv[place, :].T
        return 0

    lax.fori_loop(0, width // (2 * LANES), turn_weight, 0)

    def project(t, _):
        place = pl.ds(pl.multiple_of(t * rows, rows), rows)
        block = first[place, :]
        for low in range(0, 3 * part, wide):
            merged = nn(block, w_qkv[:, low : min(low + wide, 3 * part)]).astype(BF16)
            for q in range(merged.shape[1] // DH):
                h, kind = divmod(low // DH + q, 3)
                if kind == 1:
                    keys[h, place, :] = merged[:, q * DH : (q + 1) * DH]
        for h in range(heads):
            merged_t = nt(w_qkv_t[h * 3 * DH : (h + 1) * 3 * DH, 0:width], block).astype(BF16)
            queries_t[h, t] = (merged_t[:DH].astype(F32) * 0.125).astype(BF16)
            keys_t[h, t] = merged_t[DH : 2 * DH]
            values_t[h, t] = merged_t[2 * DH :]
        return 0

    lax.fori_loop(0, n.seq, project, 0)
    pieces[0].hand_on()
    down_gather.cross()
    for piece in pieces[2:]:
        piece.along_z()
    pieces[1].relay()

    valid, broken = r.valid_len[0], r.chain_break[0]
    exps, outs_t, inverse = r.exps, r.outs_t, r.inverse
    tiles = rows // LANES
    order = [oy * 2 + c, oy * 2 + oc, y * 2 + oc, s]

    raw = r.raw

    def tile_parts(t, tile):
        number = t * tiles + tile
        query_side = number * LANES + lax.broadcasted_iota(jnp.int32, (1, LANES), 1) >= broken
        for q in range(n.blocks):
            key_pos = q * LANES + lax.broadcasted_iota(jnp.int32, (LANES, LANES), 0)
            strip = pl.ds(pl.multiple_of((n.blocks - 1 + q - number) * LANES, LANES), LANES)
            yield slice(q * LANES, (q + 1) * LANES), strip, key_pos, (key_pos >= broken) == query_side

    def eights(array):
        return array.reshape(LANES // 8, 8, LANES)

    def attend(t):
        def one_head(h, _):
            for q in range(n.seq):
                place = slice(q * rows, (q + 1) * rows)
                raw[place, 0:rows] = nn(keys[h, place, :], queries_t[h, t])
            for tile in range(tiles):
                lanes = slice(tile * LANES, (tile + 1) * LANES)
                far_side = jnp.broadcast_to(table_line(h)[:, CLASSES - 1 : CLASSES], (1, LANES))
                top = jnp.full((8, LANES), -1e30, F32)
                for place, strip, key_pos, same in tile_parts(t, tile):
                    logits = raw[place, lanes] + jnp.where(same, bias[h, strip, :], far_side)
                    logits = jnp.where(key_pos < valid, logits, -1e30)
                    raw[place, lanes] = logits
                    top = jnp.maximum(top, jnp.max(eights(logits), axis=0))
                top = jnp.max(top, axis=0, keepdims=True)
                total = jnp.zeros((8, LANES), F32)
                for q in range(n.blocks):
                    place = slice(q * LANES, (q + 1) * LANES)
                    powers = jnp.exp(raw[place, lanes] - top)
                    total = total + jnp.sum(eights(powers), axis=0)
                    exps[h, t, place, lanes] = powers.astype(BF16)
                inverse[h, t, :, lanes] = 1.0 / jnp.sum(total, axis=0, keepdims=True)
            values_wide = jnp.concatenate([values_t[h, q] for q in range(n.seq)], axis=1)
            outs_t[h, t] = nn(values_wide, exps[h, t]) * inverse[h, t]
            return 0

        lax.fori_loop(0, heads, one_head, 0)

    mixed_first = wires.reserve(3)
    mixed_send, mixed_recv = r.mixed_send, r.mixed_recv
    mixed_sent = []
    to_send = [at_y, (d, oy * 2 + oc), at_c]
    out_gather.wait()
    out_share.start()

    def mixed_block(t):
        return jnp.concatenate([outs_t[h, t] for h in range(heads)], axis=0).T.astype(BF16)

    def send_mixed(i):
        mixed_sent.append(wires.go(mixed_first + i, mixed_send.at[i], mixed_recv.at[s], to_send[i]))

    def far_blocks(i, _):
        t = oy * 2 + lax.rem(c + i, 2)
        attend(t)
        mixed_send[i] = mixed_block(t)
        return 0

    lax.fori_loop(0, 2, far_blocks, 0)
    send_mixed(0)
    send_mixed(1)
    up_gather.hand_on()
    pieces[1].hand_on()
    down_gather.relay(0)
    out_share.hand_on()
    attend(order[2])
    mixed_send[2] = mixed_block(order[2])
    send_mixed(2)
    down_near.relay()
    attend(s)
    mixed_recv[s] = mixed_block(s)
    down_near.hand_on()

    out_share.wait_core()
    out_share.wait_last()

    def w_out(q, lanes=slice(None)):
        shards = part // n.shard
        block = r.w_out[q * shards : (q + 1) * shards, :, :, lanes]
        return block.reshape(part, block.shape[-1])

    for i in range(3):
        place = mixed_recv.at[order[i]]
        wires.make(mixed_first + i, mixed_send.at[i], place, to_send[i]).wait_recv()
    keep_hidden.wait()

    def make_branch(lanes):
        branch = nn(mixed_recv[0], w_out(0, lanes))
        for q in range(1, n.seq):
            branch = branch + nn(mixed_recv[q], w_out(q, lanes))
        r.branch[:, lanes] = branch

    by_lanes(width, make_branch)
    second_all = r.second_all
    second_gather = SeqGather(rows_of(second_all))

    def make_second(place, _):
        middle = r.hidden_own[place, :].astype(F32) + vector(gate_one) * r.branch[place, :]
        r.middle[place, :] = middle
        normal, _ = layer_norm(middle)
        r.branch_grad[place, :] = (normal * (1.0 + vector(scale_two)) + vector(shift_two)).astype(BF16)
        return 0

    by_rows(rows, make_second)
    second_all[pl.ds(pl.multiple_of(s * rows, rows), rows), :] = r.branch_grad[...]
    second_gather.start()

    own_grads.wait()
    up_gather.wait_core()
    up_gather.wait_last()
    up_gather.settle()
    feed_grads = grads_all

    def make_feed_grads(place, _):
        feed_grads[place, :] = (vector(gate_two) * grads_all[place, :].astype(F32)).astype(BF16)
        return 0

    by_rows(length, make_feed_grads)
    down_gather.relay(1)
    for piece in (pieces[0], pieces[1], down_near, down_gather):
        piece.wait()
    w_gate_up, w_down = r.w_gate_up, r.w_down
    inner, inner_t, gate_up_grads, second_t = r.inner, r.inner_t, r.gate_up_grads, r.second_t
    feed_places = (r.feed_sib, r.feed_got, r.feed_over, r.feed_come)
    feed_reduce = SeqReduce(*feed_places)
    second_reduce = SeqReduce(r.second_sib, r.second_got, r.second_over, r.second_come)
    half_hid = hid // 2

    def rows_at(t):
        return pl.ds(pl.multiple_of(t * rows, rows), rows)

    def units(t, side):
        place, low = rows_at(t), side * half_hid
        block, given = second_all[place, :], feed_grads[place, :]
        gates, ups, inner_grads = (raw.at[i * rows : (i + 1) * rows] for i in range(3))
        gates[...] = nn(block, w_gate_up[:, low : low + half_hid])
        ups[...] = nn(block, w_gate_up[:, hid + low : hid + low + half_hid])
        inner_grads[...] = nt(given, w_down[low : low + half_hid, :])
        for first_row in range(0, rows, step):
            few = slice(first_row, first_row + step)
            gate, up, inner_grad = gates[few, :], ups[few, :], inner_grads[few, :]
            sigmoid = 1.0 / (1.0 + jnp.exp(-gate))
            silu = gate * sigmoid
            to = pl.ds(pl.multiple_of(t * rows + first_row, step), step)
            inner[to, low : low + half_hid] = (silu * up).astype(BF16)
            gate_up_grads[to, low : low + half_hid] = (
                inner_grad * up * sigmoid * (1.0 + gate * (1.0 - sigmoid))
            ).astype(BF16)
            gate_up_grads[to, hid + low : hid + low + half_hid] = (inner_grad * silu).astype(BF16)

    def second_part(t, put):
        by_lanes(width, lambda lanes: put(lanes, nt(gate_up_grads[rows_at(t), :], w_gate_up[lanes, :])))

    def feed_part(t, put):
        by_lanes(width, lambda lanes: put(lanes, nn(inner[rows_at(t), :], w_down[:, lanes])), False)

    def put_in(ref):
        def put(lanes, block):
            ref[:, lanes] = block.astype(ref.dtype)

        return put

    def units_of(side):
        def one(i, _):
            units(side * 2 + lax.rem(c + i, 2), 0)
            return 0

        lax.fori_loop(0, 2, one, 0)

    second_gather.wait_core()
    units_of(y)
    second_gather.hand_on()
    pieces[2].relay()
    second_gather.wait_last()
    pieces[2].hand_on()
    pieces[3].relay()
    units_of(oy)
    pieces[3].hand_on()

    gate_up_reduces = (
        DpReduce(r.gate_up0_grad, r.gate_up0_got, r.gate_up0_come, r.gate_up0_far, r.gate_up0_mine, r.gate_up0_share),
        DpReduce(r.gate_up1_grad, r.gate_up1_got, r.gate_up1_come, r.gate_up1_far, r.gate_up1_mine, r.gate_up1_share),
    )
    down_reduce = DpReduceZ(r.down_grad, r.down_come, r.down_far, r.down_got, r.down_mine, r.down_share)
    out_reduce = DpReduce(r.proj_grad, r.proj_got, r.proj_come, r.proj_far, r.proj_mine, r.proj_share)
    qkv_reduces = (
        DpReduce(r.qkv0_grad, r.qkv0_got, r.qkv0_come, r.qkv0_far, r.qkv0_mine, r.qkv0_share),
        DpReduce(r.qkv1_grad, r.qkv1_got, r.qkv1_come, r.qkv1_far, r.qkv1_mine, r.qkv1_share),
        DpReduce(r.qkv2_grad, r.qkv2_got, r.qkv2_come, r.qkv2_far, r.qkv2_mine, r.qkv2_share),
    )

    def turn_rows(source, target):
        def turn(t, _):
            target[:, rows_at(t)] = source[rows_at(t), :].T
            return 0

        lax.fori_loop(0, n.seq, turn, 0)

    def weight_grad(left_t, right, reduce, lows):
        height, few = reduce.grad.shape[2], n.dp // 2
        columns = reduce.grad.shape[3] // len(lows)
        for at, low in enumerate(lows):
            for first_of in range(0, n.dp, few):
                grad = nn(
                    left_t[first_of * height : (first_of + few) * height, :], right[:, low : low + columns]
                ).astype(BF16)
                for i in range(few):
                    to = first_of + i
                    reduce.grad[to % 2, to // 2, :, at * columns : (at + 1) * columns] = grad[
                        i * height : (i + 1) * height
                    ]

    turn_rows(second_all, second_t)
    weight_grad(second_t, gate_up_grads, gate_up_reduces[0], (0, hid))
    gate_up_reduces[0].start()
    pieces[2].wait()
    pieces[3].wait()
    far, over, near = oy * 2 + oc, oy * 2 + c, y * 2 + oc
    units(far, 1)
    second_part(far, second_reduce.put_core(1))
    second_reduce.to_core(1)
    units(over, 1)
    second_reduce.wait_far()
    second_part(over, second_reduce.put_y())
    second_reduce.to_y()
    units(near, 1)
    second_part(near, second_reduce.put_core(0))
    second_reduce.to_core(0)
    units(s, 1)
    second_part(s, put_in(r.second_own))

    weight_grad(second_t, gate_up_grads, gate_up_reduces[1], (half_hid, hid + half_hid))
    gate_up_reduces[1].start()
    gate_up_reduces[0].along_z(3)
    turn_rows(inner, inner_t)
    weight_grad(inner_t, feed_grads, down_reduce, (0, half_hid))
    down_reduce.start(0)
    gate_up_reduces[0].along_z(1)
    down_reduce.start(1)
    feed_part(far, feed_reduce.put_core(1))
    feed_reduce.to_core(1)
    feed_part(near, feed_reduce.put_core(0))
    feed_reduce.to_core(0)
    feed_reduce.wait_far()
    feed_part(over, feed_reduce.put_y())
    feed_part(s, put_in(r.feed_own))
    lax.fori_loop(0, width // (2 * LANES), turn_weight, 0)
    values = keys

    def turn_values(t, _):
        for h in range(heads):
            values[h, rows_at(t), :] = values_t[h, t].T
        return 0

    lax.fori_loop(0, n.seq, turn_values, 0)

    sums = r.mod_sums

    upstream = r.upstream
    keep_grads.wait()
    second_reduce.wait()
    kept_middle_grad, branch_grad = r.second_own, r.branch_grad
    empty = jnp.zeros((8, width), F32)

    def put_sum(index, array):
        sums[s, :, index * width : (index + 1) * width] = jnp.sum(array, axis=0, keepdims=True)

    def second_back(place, carry):
        second_grad = second_reduce.total(r.second_own, place)
        normal, inverted = layer_norm(r.middle[place, :])
        middle_grad = upstream[place, :].astype(F32) + norm_back(
            second_grad * (1.0 + vector(scale_two)), normal, inverted
        )
        kept_middle_grad[place, :] = middle_grad
        branch_grad[place, :] = (vector(gate_one) * middle_grad).astype(BF16)
        terms = (second_grad, second_grad * normal, middle_grad * r.branch[place, :])
        return tuple(total + fold_rows(term) for total, term in zip(carry, terms))

    for index, total in zip(
        (shift_two, scale_two, gate_one), by_rows(rows, second_back, (empty, empty, empty))
    ):
        put_sum(index, total)
    back_first = wires.reserve(3)
    for copy in mixed_sent:
        wires.settle(copy)
    back_all, back_recv = mixed_send, r.back_recv
    for q in range(n.seq):
        back_all[q] = nt(branch_grad[...], w_out(q)).astype(BF16)
    for i in range(3):
        wires.go(back_first + i, back_all.at[order[i]], back_recv.at[s], to_send[i])
    back_recv[s] = back_all[s]
    feed_reduce.to_y()

    out_first = wires.reserve(2)
    second_gather.settle()
    out_parts, quarter = second_all, n.dp * n.half

    def make_out_grad(lanes):
        for q in range(n.seq):
            grad = tn(mixed_recv[q], branch_grad[:, lanes]).astype(BF16)
            for i in range(part // n.half):
                number = q * (part // n.half) + i
                low = (number % 2) * quarter + (number // 2) * n.half
                out_parts[low : low + n.half, lanes] = grad[i * n.half : (i + 1) * n.half]

    by_lanes(width, make_out_grad)

    def out_rows(core):
        return out_parts.at[pl.ds(pl.multiple_of(core * quarter, quarter), quarter)]

    lanes_oy = pl.ds(pl.multiple_of(oy * (width // 2), width // 2), width // 2)

    def out_cores():
        wires.make(out_first, out_rows(oc), r.out_near, at_c).wait_recv()
        mine = out_parts[pl.ds(pl.multiple_of(c * quarter, quarter), quarter), :]
        r.out_near[...] = (r.out_near[...].astype(F32) + mine.astype(F32)).astype(BF16)
        wires.go(out_first + 1, r.out_near.at[:, lanes_oy], r.out_far, at_y)

    def out_sum():
        wires.make(out_first + 1, r.out_near.at[:, lanes_oy], r.out_far, at_y).wait_recv()
        total = (r.out_near[:, lanes_y].astype(F32) + r.out_far[...].astype(F32)).astype(BF16)
        for to in range(n.dp):
            r.proj_grad[to % 2, to // 2] = total[to * n.half : (to + 1) * n.half]
        out_reduce.start()

    dots_t, delta = r.dots_t, r.delta
    pair_grads, query_grads = r.pair_grads, r.query_grads
    bias[...] = jnp.zeros_like(bias)
    crossed, score_grad = r.crossed, inner.at[:, 0:rows]
    crossed[...] = jnp.zeros_like(crossed)
    pair_grads[...] = jnp.zeros_like(pair_grads)
    merged_grads = gate_up_grads

    def take_back(t):
        given_t = back_recv[t].T.astype(F32)
        for h in range(heads):
            scaled = (given_t[h * DH : (h + 1) * DH] * inverse[h, t]).astype(BF16)
            dots_t[h, t] = scaled
            delta[h, t] = jnp.sum(scaled.astype(F32) * outs_t[h, t], axis=0, keepdims=True)

    def attend_back(h, t, first_of):
        place = rows_at(t)
        for q in range(n.seq):
            some = slice(q * rows, (q + 1) * rows)
            raw[some, 0:rows] = nn(values[h, some, :], dots_t[h, t])
        for tile in range(tiles):
            lanes = slice(tile * LANES, (tile + 1) * LANES)
            across = jnp.zeros((8, LANES), F32)
            for keys_of, strip, _, same in tile_parts(t, tile):
                grad = exps[h, t, keys_of, lanes].astype(F32) * (raw[keys_of, lanes] - delta[h, t, :, lanes])
                kept = jnp.where(same, grad, 0.0)
                bias[h, strip, :] = bias[h, strip, :] + kept
                across = across + jnp.sum(eights(grad - kept), axis=0)
                score_grad[keys_of, lanes] = grad.astype(BF16)
            crossed[h] = crossed[h] + jnp.sum(across, axis=0, keepdims=True)
        keys_wide = jnp.concatenate([keys_t[h, q] for q in range(n.seq)], axis=1)
        query_grads[place, :] = (nn(keys_wide, score_grad[...]) * 0.125).T.astype(BF16)
        queries, dots = queries_t[h, t].T, dots_t[h, t].T
        for q in range(n.seq):
            some = slice(q * rows, (q + 1) * rows)
            grad = jnp.concatenate([nn(score_grad[some, :], queries), nn(exps[h, t, some, :], dots)], axis=1)
            pair_grads[some, :] = grad if first_of else pair_grads[some, :] + grad

    def end_head(h):
        for q in range(n.seq):
            some = slice(q * rows, (q + 1) * rows)
            merged_grads[some, h * wide : h * wide + 3 * DH] = jnp.concatenate(
                [query_grads[some, :], pair_grads[some, :].astype(BF16)], axis=1
            )
        merged = merged_grads.at[:, h * wide : h * wide + 3 * DH]
        totals = nn(jnp.ones((16, length), BF16), merged[...])[0:1]
        few = n.dp // 2 * n.shard
        for first_of in range(0, width, few):
            place = slice(first_of, first_of + few)
            scale, shift = 1.0 + r.mod_t[place, 1:2], r.mod_t[place, 0:1]
            weights = w_qkv[place, h * 3 * DH : (h + 1) * 3 * DH].astype(F32)
            product = nn(r.norm_t[place, :], merged[...])
            d_shift = jnp.sum(weights * totals, axis=1, keepdims=True)
            d_scale = jnp.sum(weights * product, axis=1, keepdims=True)
            lane = lax.broadcasted_iota(jnp.int32, (few, LANES), 1)
            both = jnp.where(lane == 0, d_shift, jnp.where(lane == 1, d_scale, 0.0))
            r.first_sums[place, :] = both if h == 0 else r.first_sums[place, :] + both
            grad = (product * scale + totals * shift).astype(BF16)
            for i in range(n.dp // 2):
                to = first_of // n.shard + i
                low = i * n.shard
                qkv_reduces[h].grad[to % 2, to // 2] = jnp.concatenate(
                    [grad[low : low + n.half], grad[low + n.half : low + n.shard]], axis=1
                )
        qkv_reduces[h].start()

    def back_block(i):
        wires.make(back_first + i, back_recv.at[order[i]], back_recv.at[order[i]], to_send[i]).wait_recv()
        take_back(order[i])

    def some_of_head(h, side):
        def one(i, _):
            attend_back(h, side * 2 + lax.rem(c + i, 2), False)
            return 0

        lax.fori_loop(0, 2, one, 0)

    def rest_of_head(h):
        pair_grads[...] = jnp.zeros_like(pair_grads)

        def one(i, _):
            attend_back(h, lax.rem(y + i // 2, 2) * 2 + lax.rem(c + lax.rem(i, 2), 2), False)
            return 0

        lax.fori_loop(0, n.seq, one, 0)

    wires.go(out_first, out_rows(oc), r.out_near, at_c)
    gate_up_reduces[0].along_z(2)
    gate_up_reduces[0].along_z(0)
    gate_up_reduces[1].along_z(3)
    take_back(s)
    back_block(2)
    some_of_head(0, y)
    gate_up_reduces[1].along_z(1)
    out_cores()
    back_block(0)
    back_block(1)
    some_of_head(0, oy)
    end_head(0)
    rest_of_head(1)
    end_head(1)
    down_reduce.merge()
    rest_of_head(2)
    end_head(2)

    second_reduce.settle()
    first_reduce = SeqReduce(r.second_sib, r.second_got, r.second_over, r.second_come)

    def first_part(t, put):
        def by_heads(lanes):
            total = nn(merged_grads[rows_at(t), 0 : 3 * DH], w_qkv_t[0 : 3 * DH, lanes])
            for h in range(1, heads):
                total = total + nn(
                    merged_grads[rows_at(t), h * wide : h * wide + 3 * DH],
                    w_qkv_t[h * 3 * DH : (h + 1) * 3 * DH, lanes],
                )
            put(lanes, total)

        by_lanes(width, by_heads)

    first_part(oy * 2 + oc, first_reduce.put_core(1))
    first_reduce.to_core(1)
    first_reduce.wait_far()
    first_part(oy * 2 + c, first_reduce.put_y())
    first_reduce.to_y()
    first_part(y * 2 + oc, first_reduce.put_core(0))
    first_reduce.to_core(0)
    first_part(s, put_in(r.branch))
    gate_up_reduces[1].along_z(2)
    gate_up_reduces[1].along_z(0)
    for k in (3, 1, 2, 0):
        qkv_reduces[0].along_z(k)
    qkv_reduces[1].along_z(3)
    feed_reduce.wait()

    def make_result(place, total):
        feed = feed_reduce.total(r.feed_own, place)
        r.result[place, :] = (r.middle[place, :] + vector(gate_two) * feed).astype(BF16)
        return total + fold_rows(upstream[place, :].astype(F32) * feed)

    put_sum(gate_two, by_rows(rows, make_result, empty))
    turned = r.first_sums[...].T
    put_sum(shift_one, turned[0:1])
    put_sum(scale_one, turned[1:2])
    sums_first = wires.reserve(3)
    for i, (a, b) in enumerate(seq_peers):
        wires.go(sums_first + i, sums.at[s], sums.at[s], (d, seq_peer(a, b)))
    qkv_reduces[1].along_z(1)
    down_reduce.across()
    qkv_reduces[2].along_z(3)
    qkv_reduces[1].along_z(2)
    qkv_reduces[1].along_z(0)
    out_sum()
    qkv_reduces[2].along_z(1)

    table_sums, table_all = r.table_sums, r.table_all

    def fold(h, _):
        lane = lax.broadcasted_iota(jnp.int32, (1, LANES), 1)
        near = jnp.zeros((LANES, LANES), F32)
        low_end = jnp.zeros((LANES, LANES), F32)
        high_end = jnp.zeros((LANES, LANES), F32)
        for tile in range(2 * n.blocks - 1):
            away = tile - middle_tile
            apart = query_in - key_in - away * LANES
            value = bias[h, tile * LANES : (tile + 1) * LANES]
            if away < -1:
                high_end = high_end + value
            elif away > 1:
                low_end = low_end + value
            else:
                high_end = high_end + jnp.where(apart >= RR, value, 0.0)
                low_end = low_end + jnp.where(apart <= -RR, value, 0.0)
                near = near + jnp.where((apart < RR) & (apart > -RR), value, 0.0)
        line = jnp.sum(skew(near, True), axis=0, keepdims=True)
        for where, array in ((40, low_end), (41, high_end), (42, crossed[h])):
            line = jnp.where(lane == where, jnp.sum(array), line)
        table_sums[d, h] = line
        return 0

    lax.fori_loop(0, heads, fold, 0)
    table_first = wires.reserve(len(dp_peers))
    for i, (k, e) in enumerate(dp_peers):
        wires.go(table_first + i, table_sums.at[d], table_sums.at[d], (dp_peer(k, e)[0], s))

    for i, (a, b) in enumerate(seq_peers):
        place = sums.at[seq_peer(a, b)]
        wires.make(sums_first + i, place, place, (d, seq_peer(a, b))).wait_recv()
    mod_total = sums[0]
    for i in range(1, n.seq):
        mod_total = mod_total + sums[i]
    mod_totals = r.mod_totals
    mod_totals[d] = mod_total
    totals_first = wires.reserve(len(dp_peers))
    for i, (k, e) in enumerate(dp_peers):
        wires.go(totals_first + i, mod_totals.at[d], mod_totals.at[d], (dp_peer(k, e)[0], s))
    qkv_reduces[2].along_z(2)
    qkv_reduces[2].along_z(0)
    gate_up_reduces[0].finish()
    gate_up_reduces[1].finish()
    down_reduce.finish()
    out_reduce.along_z(3)
    first_reduce.wait()

    def first_back(place, _):
        first_grad = first_reduce.total(r.branch, place)
        normal, inverted = layer_norm(r.hidden_own[place, :].astype(F32))
        r.input_grad[place, :] = (
            kept_middle_grad[place, :] + norm_back(first_grad * (1.0 + vector(scale_one)), normal, inverted)
        ).astype(BF16)
        return 0

    by_rows(rows, first_back)
    for k in (1, 2, 0):
        out_reduce.along_z(k)
    for reduce in qkv_reduces:
        reduce.finish()
    for reduce in (*gate_up_reduces, down_reduce):
        reduce.shares.hand_on()
    for i, (k, e) in enumerate(dp_peers):
        place = table_sums.at[dp_peer(k, e)[1]]
        wires.make(table_first + i, place, place, (dp_peer(k, e)[0], s)).wait_recv()
    total = table_sums[0]
    for i in range(1, n.dp):
        total = total + table_sums[i]
    table_all[s] = total
    table_second = wires.reserve(3)
    for i, (a, b) in enumerate(seq_peers):
        wires.go(table_second + i, table_all.at[s], table_all.at[s], (d, seq_peer(a, b)))
    out_reduce.finish()
    for i, (k, e) in enumerate(dp_peers):
        place = mod_totals.at[dp_peer(k, e)[1]]
        wires.make(totals_first + i, place, place, (dp_peer(k, e)[0], s)).wait_recv()
    squashed_rows = r.squashed[pl.ds(pl.multiple_of(d * n.ada_rows, n.ada_rows), n.ada_rows), :]
    ada = squashed_rows[:, 0:1] * mod_totals[0]
    for i in range(1, n.dp):
        ada = ada + squashed_rows[:, i : i + 1] * mod_totals[i]
    r.grad_ada[...] = ada
    for i, (a, b) in enumerate(seq_peers):
        place = table_all.at[seq_peer(a, b)]
        wires.make(table_second + i, place, place, (d, seq_peer(a, b))).wait_recv()
    r.table[...] = table_all[...]
    for reduce in (*qkv_reduces, out_reduce):
        reduce.shares.hand_on()
    for reduce in (*gate_up_reduces, down_reduce, *qkv_reduces, out_reduce):
        reduce.shares.wait()
    wires.finish()


def write_outputs(sizes, inputs, outputs):
    n = sizes
    result, input_grad, grad_ada, table, gate_up0, gate_up1, down, proj, qkv0, qkv1, qkv2 = inputs[:-3]
    pair_embed, pair_gain, pair_weight = inputs[-3:]
    o_result, o_input, o_qkv, o_out, o_gate_up, o_down, o_ada, o_embed, o_gain, o_pair = outputs
    o_result[...] = result[...]
    o_input[...] = input_grad[...]
    o_ada[...] = grad_ada[...]
    everyone = range(n.seq)
    for kind in range(3):
        for side in range(2):
            low = (3 * side + kind) * DH
            o_qkv[side * n.half : (side + 1) * n.half, kind * n.width : (kind + 1) * n.width] = jnp.concatenate(
                [head[q, :, low : low + DH] for q in everyone for head in (qkv0, qkv1, qkv2)], axis=1
            ).astype(F32)
    group = n.seq * n.strip
    for number in range(2 * n.dp):
        side, block = divmod(number % n.dp, n.dp // 2)
        low = (number // n.dp) * (n.hidden // 2) + block * n.strip
        gate_up = (gate_up0, gate_up1)[side]
        o_gate_up[:, number * group : (number + 1) * group] = jnp.concatenate(
            [gate_up[q, :, low : low + n.strip] for q in everyone], axis=1
        ).astype(F32)
    for q in everyone:
        o_down[q * n.strip : (q + 1) * n.strip, :] = down[q].astype(F32)
        side, core = divmod(q, 2)
        lanes = slice(side * (n.width // 2), (side + 1) * (n.width // 2))
        o_out[core * n.half : (core + 1) * n.half, lanes] = proj[q].astype(F32)

    lines = jnp.concatenate([table[q, h] for q in everyone for h in range(n.heads)], axis=0)
    lane = lax.broadcasted_iota(jnp.int32, lines.shape, 1)
    table_t = jnp.where(lane < 2 * RR, pltpu.roll(lines, RR, 1), 0.0)
    for number, at in ((0, 40), (2 * RR, 41), (CLASSES - 1, 42)):
        table_t = jnp.where(lane == number, jnp.broadcast_to(lines[:, at : at + 1], lines.shape), table_t)
    embed = pair_embed[...].astype(F32)
    embed = jnp.concatenate([embed, jnp.zeros((LANES - CLASSES, embed.shape[1]), F32)], axis=0)
    gain = pair_gain[...].astype(F32)
    normal, inverted = layer_norm(embed, 1e-05)

    def exact(a, b):
        return jnp.dot(a, b, precision=HIGHEST, preferred_element_type=F32)

    o_pair[...] = exact(table_t, normal * gain)
    scaled_grad = exact(table_t.T, pair_weight[...].astype(F32))
    o_gain[...] = jnp.sum(scaled_grad * normal, axis=0)
    o_embed[...] = norm_back(scaled_grad * gain, normal, inverted)[0:CLASSES]


def fused_layer(
    sizes, valid_len, chain_break, hidden, out_grad, condition, qkv, out, gate_up, down, ada, embed, gain, weight
):
    n = sizes
    rows, width, length, heads, part, hid = n.rows, n.width, n.length, n.heads, n.part, n.hidden
    any_space, vmem, smem = pl.ANY, pltpu.VMEM, pltpu.SMEM
    inputs = dict(
        valid_len=(valid_len, smem),
        chain_break=(chain_break, smem),
        hidden=(hidden, any_space),
        out_grad=(out_grad, any_space),
        condition=(condition, vmem),
        qkv=(qkv, any_space),
        out=(out, any_space),
        gate_up=(gate_up, any_space),
        down=(down, any_space),
        ada=(ada, vmem),
        pair_embed=(embed, vmem),
        pair_gain=(gain, vmem),
        pair_weight=(weight, vmem),
    )
    modulations = 6 * width

    def reduced(height, columns):
        return (
            ((2, n.far, height, columns), BF16),
            ((n.far, height, columns), BF16),
            ((n.far - 1, height, columns), BF16),
            ((height, columns), BF16),
            ((height, columns), BF16),
        )

    def shares(height, columns):
        return (n.seq, height, columns), BF16, any_space

    sums = ((2, rows, width), BF16), ((2, rows, width), BF16), ((rows, width), BF16), ((rows, width), BF16)
    gate_up_sizes, down_sizes = (n.shard, hid), (n.strip, width)
    proj_sizes, qkv_sizes = (n.half, width // 2), (n.half, 6 * DH)
    outputs = dict(
        result=((rows, width), BF16, vmem),
        input_grad=((rows, width), BF16, vmem),
        grad_ada=((n.ada_rows, modulations), F32, vmem),
        table=((n.seq, heads, 1, LANES), F32, vmem),
        gate_up0_share=shares(*gate_up_sizes),
        gate_up1_share=shares(*gate_up_sizes),
        down_share=shares(*down_sizes),
        proj_share=shares(*proj_sizes),
        qkv0_share=shares(*qkv_sizes),
        qkv1_share=shares(*qkv_sizes),
        qkv2_share=shares(*qkv_sizes),
    )
    scratch = dict(
        w_qkv=((width, 3 * part), BF16),
        w_out=((n.dp, 2, n.half, width), BF16),
        w_gate_up=((width, 2 * hid), BF16),
        w_down=((hid, width), BF16),
        hidden_all=((length, width), BF16),
        grads_all=((length, width), BF16),
        hidden_own=((rows, width), BF16),
        upstream=((rows, width), BF16),
        cond_all=((n.dp, 8, n.conditioning), F32),
        squashed=((n.conditioning, n.dp), F32),
        mod_send=((n.dp, 1, modulations), F32),
        mod_recv=((n.dp, 1, modulations), F32),
        modulation=((1, modulations), F32),
        mod_sums=((n.seq, 1, modulations), F32),
        mod_totals=((n.dp, 1, modulations), F32),
        bias=((heads, (2 * n.blocks - 1) * LANES, LANES), F32),
        crossed=((heads, 1, LANES), F32),
        table_t=((H, LANES), F32),
        table_sums=((n.dp, heads, 1, LANES), F32),
        table_all=((n.seq, heads, 1, LANES), F32),
        keys=((heads, length, DH), BF16),
        keys_t=((heads, n.seq, DH, rows), BF16),
        values_t=((heads, n.seq, DH, rows), BF16),
        queries_t=((heads, n.seq, DH, rows), BF16),
        exps=((heads, n.seq, length, rows), BF16),
        outs_t=((heads, n.seq, DH, rows), F32),
        inverse=((heads, n.seq, 1, rows), F32),
        mixed_send=((n.seq, rows, part), BF16),
        mixed_recv=((n.seq, rows, part), BF16),
        back_recv=((n.seq, rows, part), BF16),
        branch=((rows, width), F32),
        middle=((rows, width), F32),
        feed_own=((rows, width), F32),
        second_own=((rows, width), F32),
        branch_grad=((rows, width), BF16),
        second_all=((length, width), BF16),
        second_t=((width, length), BF16),
        norm_t=((width, length), BF16),
        mod_t=((width, 8), F32),
        first_sums=((width, LANES), F32),
        inner=((length, hid), BF16),
        inner_t=((hid, length), BF16),
        gate_up_grads=((length, 2 * hid), BF16),
        out_near=((n.dp * n.half, width), BF16),
        out_far=((n.dp * n.half, width // 2), BF16),
        raw=((length, hid // 2), F32),
        dots_t=((heads, n.seq, DH, rows), BF16),
        delta=((heads, n.seq, 1, rows), F32),
        pair_grads=((length, 2 * DH), F32),
        query_grads=((length, DH), BF16),
        feed_sib=sums[0],
        feed_got=sums[1],
        feed_over=sums[2],
        feed_come=sums[3],
        second_sib=sums[0],
        second_got=sums[1],
        second_over=sums[2],
        second_come=sums[3],
        gate_up0_grad=reduced(*gate_up_sizes)[0],
        gate_up0_got=reduced(*gate_up_sizes)[1],
        gate_up0_come=reduced(*gate_up_sizes)[2],
        gate_up0_far=reduced(*gate_up_sizes)[3],
        gate_up0_mine=reduced(*gate_up_sizes)[4],
        gate_up1_grad=reduced(*gate_up_sizes)[0],
        gate_up1_got=reduced(*gate_up_sizes)[1],
        gate_up1_come=reduced(*gate_up_sizes)[2],
        gate_up1_far=reduced(*gate_up_sizes)[3],
        gate_up1_mine=reduced(*gate_up_sizes)[4],
        proj_grad=reduced(*proj_sizes)[0],
        proj_got=reduced(*proj_sizes)[1],
        proj_come=reduced(*proj_sizes)[2],
        proj_far=reduced(*proj_sizes)[3],
        proj_mine=reduced(*proj_sizes)[4],
        qkv0_grad=reduced(*qkv_sizes)[0],
        qkv0_got=reduced(*qkv_sizes)[1],
        qkv0_come=reduced(*qkv_sizes)[2],
        qkv0_far=reduced(*qkv_sizes)[3],
        qkv0_mine=reduced(*qkv_sizes)[4],
        qkv1_grad=reduced(*qkv_sizes)[0],
        qkv1_got=reduced(*qkv_sizes)[1],
        qkv1_come=reduced(*qkv_sizes)[2],
        qkv1_far=reduced(*qkv_sizes)[3],
        qkv1_mine=reduced(*qkv_sizes)[4],
        qkv2_grad=reduced(*qkv_sizes)[0],
        qkv2_got=reduced(*qkv_sizes)[1],
        qkv2_come=reduced(*qkv_sizes)[2],
        qkv2_far=reduced(*qkv_sizes)[3],
        qkv2_mine=reduced(*qkv_sizes)[4],
        down_grad=reduced(*down_sizes)[0],
        down_come=((n.far - 1, 2, *down_sizes), BF16),
        down_far=((2, *down_sizes), BF16),
        down_got=(down_sizes, BF16),
        down_mine=(down_sizes, BF16),
    )
    semaphores = dict(send_sem=210, recv_sem=210, local_sem=21)
    names = [*inputs, *outputs, *scratch, *semaphores]
    made = pl.pallas_call(
        functools.partial(layer_kernel, n, names),
        out_shape=[jax.ShapeDtypeStruct(shape, kind) for shape, kind, _ in outputs.values()],
        in_specs=[pl.BlockSpec(memory_space=space) for _, space in inputs.values()],
        out_specs=[pl.BlockSpec(memory_space=space) for _, _, space in outputs.values()],
        scratch_shapes=[pltpu.VMEM(shape, kind) for shape, kind in scratch.values()]
        + [pltpu.SemaphoreType.DMA((count,)) for count in semaphores.values()],
        compiler_params=pltpu.CompilerParams(
            collective_id=0, has_side_effects=True, vmem_limit_bytes=VMEM_LIMIT
        ),
    )(*[array for array, _ in inputs.values()])
    gradients = (
        ((rows, width), BF16),
        ((rows, width), BF16),
        ((n.shard, 3 * width), F32),
        ((n.shard, width), F32),
        ((n.shard, 2 * n.seq * hid), F32),
        ((n.seq * n.strip, width), F32),
        ((n.ada_rows, modulations), F32),
        (embed.shape, F32),
        (gain.shape, F32),
        (weight.shape, F32),
    )
    count = len(made) + 3

    def write(*refs):
        write_outputs(n, refs[:count], refs[count:])

    return pl.pallas_call(
        write,
        out_shape=[jax.ShapeDtypeStruct(shape, kind) for shape, kind in gradients],
        in_specs=[pl.BlockSpec(memory_space=vmem)] * count,
        out_specs=[pl.BlockSpec(memory_space=vmem)] * len(gradients),
        compiler_params=pltpu.CompilerParams(vmem_limit_bytes=VMEM_LIMIT),
    )(*made, embed, gain, weight)


def fused_body(
    hidden_in,
    condition,
    qkv_weight,
    out_weight,
    gate_up_weight,
    down_weight,
    ada_weight,
    pair_embed,
    pair_gain,
    pair_weight,
    valid_len,
    chain_break,
    out_grad,
):
    _, rows, width = hidden_in.shape
    seq = lax.axis_size("seq")
    dp = lax.axis_size("dp")
    shard = qkv_weight.shape[0]
    sizes = Sizes(
        rows, width, seq, dp, shard, down_weight.shape[0], ada_weight.shape[0], condition.shape[1]
    )
    outs = fused_layer(
        sizes,
        valid_len,
        chain_break,
        hidden_in[0],
        out_grad[0],
        condition,
        qkv_weight,
        out_weight,
        gate_up_weight,
        down_weight,
        ada_weight,
        pair_embed,
        pair_gain,
        pair_weight.T,
    )
    result, input_grad, *grads, grad_gain, grad_pair = outs
    return (result[None], input_grad[None], *grads, grad_gain, grad_pair.T)


def body(*arguments):
    hidden_in, _, qkv_weight, _, _, down_weight = arguments[:6]
    seq, dp = lax.axis_size("seq"), lax.axis_size("dp")
    whole_tiles = qkv_weight.shape[0] % 32 == 0 and down_weight.shape[0] % (16 * seq) == 0
    if whole_tiles and hidden_in.shape[0] == 1 and seq == 4 and dp == 8:
        return fused_body(*arguments)
    return plain_body(*arguments)


def solution(mesh):
    rows = P("dp", "seq", None)
    share = P("dp", None)
    return jax.shard_map(
        body,
        mesh=mesh,
        in_specs=(rows, share, share, share, share, share, share, P(), P(), P(), P("dp"), P("dp"), rows),
        out_specs=(rows, rows, share, share, share, share, share, P(), P(), P()),
        check_vma=False,
    )
```

profile of v0, /device:TPU:0, one launch (start us, length us, event | category | flops | bytes accessed | tf_op | source)
XLA Modules:
  0.0 161.1 jit_solution(2384699642837931836)
XLA Ops:
  1.9 153.3 %shard_map.204 = (bf16[256,768]{1,0:T(8,128)(2,1)}, bf16[256,768]{1,0:T(8,128)(2,1)}, f32[32,4608]{1,0:T(8,128)}, f32[4,3,1,128]{3,2,1,0:T(1,128)}, bf16[4,96,76...) custom-call(s32[1]{0:T(128)S(6)} %copy.23.refs_0_, ...), custom_call_target="tpu_custom_call" | custom-call | tf_op jit(solution)/shard_map/pallas_call | solution.py:1674
  155.2 5.6 %shard_map.205 = (bf16[256,768]{1,0:T(8,128)(2,1)}, bf16[256,768]{1,0:T(8,128)(2,1)}, f32[96,2304]{1,0:T(8,128)}, f32[96,768]{1,0:T(8,128)}, f32[96,6144]{1,0:T(...) custom-call(bf16[256,768]{1,0:T(8,128)(2,1)} %get-tuple-element.31.r, ...), custom_call_target="tpu_custom_call" | custom-call | tf_op jit(solution)/shard_map/pallas_call | solution.py:1702
where the time goes:
time: 162 us; the launch traced here: 161 us
  Pallas kernels  159 us (98%)
  between operations  2.14 us (1%)
    pallas_call x1, Pallas kernels, fused_layer(): pl.pallas_call(functools.partial(layer_kernel, n, names), out_shape=[jax....  153 us
    pallas_call x1, Pallas kernels, fused_layer(): pl.pallas_call(write, out_shape=[jax.ShapeDtypeStruct(shape, kind) for sh...  5.65 us

commit v1 on v0

--- a/solution.py
+++ b/solution.py
@@ -1313,18 +1313,18 @@
         lax.fori_loop(0, n.seq, one, 0)
 
     wires.go(out_first, out_rows(oc), r.out_near, at_c)
-    gate_up_reduces[0].along_z(2)
     gate_up_reduces[0].along_z(0)
     gate_up_reduces[1].along_z(3)
     take_back(s)
     back_block(2)
     some_of_head(0, y)
-    gate_up_reduces[1].along_z(1)
+    gate_up_reduces[0].along_z(2)
     out_cores()
     back_block(0)
     back_block(1)
     some_of_head(0, oy)
     end_head(0)
+    gate_up_reduces[1].along_z(1)
     rest_of_head(1)
     end_head(1)
     down_reduce.merge()

time: 162 us -> 162 us (level)
  no operation moved by 1% of the time
where the time goes in v1:
time: 162 us; the launch traced here: 161 us
  Pallas kernels  159 us (98%)
  between operations  2.14 us (1%)
    pallas_call x1, Pallas kernels, fused_layer(): pl.pallas_call(functools.partial(layer_kernel, n, names), out_shape=[jax....  153 us
    pallas_call x1, Pallas kernels, fused_layer(): pl.pallas_call(write, out_shape=[jax.ShapeDtypeStruct(shape, kind) for sh...  5.65 us

profile of v1, /device:TPU:0, one launch (start us, length us, event | category | flops | bytes accessed | tf_op | source)
XLA Modules:
  0.0 161.1 jit_solution(6267269523816306871)
XLA Ops:
  1.9 153.3 %shard_map.204 = (bf16[256,768]{1,0:T(8,128)(2,1)}, bf16[256,768]{1,0:T(8,128)(2,1)}, f32[32,4608]{1,0:T(8,128)}, f32[4,3,1,128]{3,2,1,0:T(1,128)}, bf16[4,96,76...) custom-call(s32[1]{0:T(128)S(6)} %copy.23.refs_0_, ...), custom_call_target="tpu_custom_call" | custom-call | tf_op jit(solution)/shard_map/pallas_call | solution.py:1674
  155.3 5.6 %shard_map.205 = (bf16[256,768]{1,0:T(8,128)(2,1)}, bf16[256,768]{1,0:T(8,128)(2,1)}, f32[96,2304]{1,0:T(8,128)}, f32[96,768]{1,0:T(8,128)}, f32[96,6144]{1,0:T(...) custom-call(bf16[256,768]{1,0:T(8,128)(2,1)} %get-tuple-element.31.r, ...), custom_call_target="tpu_custom_call" | custom-call | tf_op jit(solution)/shard_map/pallas_call | solution.py:1702
